TPU v7x, 512 devices: a whole 4x4x16 slice. The times are simulated.
512 devices in a mesh: users: 64 (over y, z_lo, core), items: 8 (over x, z_hi).
Axes of the slice: x: 4, y: 4, z: 16 (z_hi: 2, z_lo: 8; z = z_hi * 8 + z_lo), core: 2. Of those that a mesh axis runs over, the one named last changes fastest.
Arguments:
- interactions: bfloat16 [3, 81920, 2048], P(None, 'users', 'items')
- matchings: int32 [3], replicated, may hold values from 1 to 63, as said below
- user_shape: bfloat16 [81920, 128], P('users'), may hold values from 0.5 to 2
- item_shape: bfloat16 [131072, 128], P(('users', 'items')), may hold values from 0.5 to 2
Outputs:
- user_log: bfloat16 [81920, 128], P('users')
- item_log: bfloat16 [131072, 128], P(('users', 'items'))
Inputs may be any that keep to these rules, and one draw needn't show every extreme that they name: matchings[0] and matchings[1] are two different values of 1 to 62, and the last matching is 63.
All inputs are finite; a program needn't handle non-finite values.
Results may differ from a plain program's by a relative error of at most 0.0012.
The roundings to bfloat16 on the way count: a program that leaves them out, or rounds other values in their place, can miss the bound.
Values sent between devices are 32-bit elements; how exact they have to be, the bound alone decides.
A program may use at most 64 MiB of HBM per device.

v0:
```python
import jax
import jax.numpy as jnp
from jax import lax
from jax.sharding import PartitionSpec as P

STRATA = 3


def swapped(value, axis, stride):
    mask = 2**stride
    pairs = [(source, source ^ mask) for source in range(lax.axis_size(axis))]
    return lax.ppermute(value, axis, pairs)


def expect(shp, rte):
    return (lax.digamma(shp) - jnp.log(rte), shp / rte)


def bit_sequence(bit_count):
    ascending = list(range(bit_count))
    return ascending


def chosen_bit(target, bit):
    return target // 2**bit % 2 == 1


def route_with(first, second, target, bit_count, mover):
    for bit in bit_sequence(bit_count):
        picked = chosen_bit(target, bit)
        copy_first, copy_second = mover((first, second), bit)
        first = jnp.where(picked, copy_first, first)
        second = jnp.where(picked, copy_second, second)
    return (first, second)


def mover_out(pair, bit):
    return swapped((pair[0], pair[1]), "users", bit)


def mover_back(pair, bit):
    return swapped((pair[0], pair[1]), "users", bit)


def per_device(interactions, matchings, user_shape, item_shape):
    group_size = lax.axis_size("users")
    bit_count = group_size.bit_length() - 1
    factor_users = float(group_size)
    user_shp = user_shape.astype(jnp.float32)
    user_rte = jnp.ones_like(user_shp)
    item_shp = item_shape.astype(jnp.float32)
    item_rte = jnp.ones_like(item_shp)
    visit_shp, visit_rte = (item_shp, item_rte)
    for stratum in range(STRATA):
        target = matchings[stratum]
        visit_shp, visit_rte = route_with(item_shp, item_rte, target, bit_count, mover_out)
        user_elog, user_mean = expect(user_shp, user_rte)
        item_elog, item_mean = expect(visit_shp, visit_rte)
        user_exp = jnp.exp(user_elog).astype(jnp.bfloat16)
        item_exp = jnp.exp(item_elog).astype(jnp.bfloat16)
        denominator = lax.dot_general(
            user_exp, item_exp, (((1,), (1,)), ((), ())), preferred_element_type=jnp.float32
        )
        ratios = (interactions[stratum].astype(jnp.float32) / denominator).astype(jnp.bfloat16)
        user_local = user_exp.astype(jnp.float32) * jnp.dot(
            ratios, item_exp, preferred_element_type=jnp.float32
        )
        item_stat = item_exp.astype(jnp.float32) * lax.dot_general(
            ratios, user_exp, (((0,), (0,)), ((), ())), preferred_element_type=jnp.float32
        )
        beta_cols = jnp.sum(item_mean, axis=0)
        theta_cols = jnp.sum(user_mean, axis=0)
        user_stat, beta_total = lax.psum((user_local, beta_cols), "items")
        user_shp = 0.5 * user_shp + 0.5 * (0.3 + factor_users * user_stat)
        user_rte = 0.5 * user_rte + 0.5 * (0.3 + factor_users * beta_total[None, :])
        back_stat, back_cols = route_with(item_stat, theta_cols, target, bit_count, mover_back)
        item_shp = 0.5 * item_shp + 0.5 * (0.3 + factor_users * back_stat)
        item_rte = 0.5 * item_rte + 0.5 * (0.3 + factor_users * back_cols[None, :])
    user_log = (lax.digamma(user_shp) - jnp.log(user_rte)).astype(jnp.bfloat16)
    item_log = (lax.digamma(item_shp) - jnp.log(item_rte)).astype(jnp.bfloat16)
    return (user_log, item_log)


def solution(mesh):
    placed = (P(None, "users", "items"), P(), P("users", None), P(("users", "items"), None))
    return jax.shard_map(
        per_device,
        mesh=mesh,
        in_specs=placed,
        out_specs=(P("users", None), P(("users", "items"), None)),
        check_vma=False,
    )
```

profile of v0, /device:TPU:1, one launch (start us, length us, event | category | flops | bytes accessed | tf_op | source)
XLA Modules:
  0.0 961.7 jit_solution(8319633222621084648)
XLA Ops:
  7.2 8.8 collective-permute-start.6
  35.8 7.5 collective-permute-done.8
  46.2 6.4 collective-permute-start.3
  52.6 16.3 %collective-permute-done.9 = f32[256,128]{1,0:T(8,128)S(1)} collective-permute-done((f32[256,128]{1,0:T(8,128)S(1)}, f32[256,128]{1,0:T(8,128)S(1)}, u32[]{:S(2)}, u32[]{:S(2)}) %collective-permute-start.9) | collective-permute-done | bytes 131104 | tf_op jit(solution)/shard_map/ppermute | solution.py:12
  82.2 4.7 fusion.6
  89.7 4.8 collective-permute-start.12
  100.6 42.1 %psum.43 = f32[128]{0:T(128)S(1)} all-reduce(f32[128]{0:T(128)S(1)} %get-tuple-element.21), channel_id=1, replica_groups=mesh['users'=64,'items'=8] {'items'}, use_global_device_ids=true, to_apply=%region_2.3 | all-reduce | flops 128 | bytes 1024 | tf_op jit(solution)/shard_map/psum | solution.py:73
  144.7 18.0 %collective-permute-done.14 = f32[256,128]{1,0:T(8,128)S(1)} collective-permute-done((f32[256,128]{1,0:T(8,128)S(1)}, f32[256,128]{1,0:T(8,128)S(1)}, u32[]{:S(2)}, u32[]{:S(2)}) %collective-permute-start.14) | collective-permute-done | bytes 131104 | tf_op jit(solution)/shard_map/ppermute | solution.py:12
  164.6 135.7 %all-reduce.5.cloned.1.call-done = f32[1280,128]{1,0:T(8,128)} async-done(((f32[1280,128]{1,0:T(8,128)}), f32[1280,128]{1,0:T(8,128)}) %all-reduce.5.cloned.1.call-update) | async-done | bytes 655376 | tf_op jit(solution)/shard_map/psum | solution.py:73
  300.3 5.8 divide_reduce_fusion.1
  326.5 5.6 collective-permute-start.51
  353.8 5.5 collective-permute-start.30
  377.9 6.0 collective-permute-done.32
  387.7 5.5 collective-permute-start.21
  393.1 17.7 %collective-permute-done.33 = f32[256,128]{1,0:T(8,128)S(1)} collective-permute-done((f32[256,128]{1,0:T(8,128)S(1)}, f32[256,128]{1,0:T(8,128)S(1)}, u32[]{:S(2)}, u32[]{:S(2)}) %collective-permute-start.33) | collective-permute-done | bytes 131104 | tf_op jit(solution)/shard_map/ppermute | solution.py:12
  431.1 4.8 collective-permute-start.36
  438.9 4.7 collective-permute-done.37
  445.5 9.0 collective-permute-done.38
  456.5 14.7 %collective-permute-done.39 = f32[256,128]{1,0:T(8,128)S(1)} collective-permute-done((f32[256,128]{1,0:T(8,128)S(1)}, f32[256,128]{1,0:T(8,128)S(1)}, u32[]{:S(2)}, u32[]{:S(2)}) %collective-permute-start.39) | collective-permute-done | bytes 131104 | tf_op jit(solution)/shard_map/ppermute | solution.py:12
  502.5 7.6 collective-permute-done.56
  512.9 6.4 collective-permute-start.45
  519.3 14.6 %collective-permute-done.57 = f32[256,128]{1,0:T(8,128)S(1)} collective-permute-done((f32[256,128]{1,0:T(8,128)S(1)}, f32[256,128]{1,0:T(8,128)S(1)}, u32[]{:S(2)}, u32[]{:S(2)}) %collective-permute-start.57) | collective-permute-done | bytes 131104 | tf_op jit(solution)/shard_map/ppermute | solution.py:12
  552.2 38.0 %all-reduce = (f32[128]{0:T(128)S(1)}, f32[128]{0:T(128)S(1)}) all-reduce(f32[128]{0:T(128)S(1)} %get-tuple-element.19, f32[128]{0:T(128)S(1)} %get-tuple-element.17), channel_id=1, replica_groups=mesh['users'=64,'items'=8] {'items'}, use_global_device_ids=true, to_apply=%region_6.7 | all-reduce | flops 256 | bytes 2048 | tf_op jit(solution)/shard_map/psum | solution.py:73
  590.1 152.1 %all-reduce.7.cloned.1.call-done = f32[1280,128]{1,0:T(8,128)} async-done(((f32[1280,128]{1,0:T(8,128)}), f32[1280,128]{1,0:T(8,128)}) %all-reduce.7.cloned.1.call-update) | async-done | bytes 655376 | tf_op jit(solution)/shard_map/psum | solution.py:73
  746.6 4.7 fusion.16
  765.6 6.5 collective-permute-start.69
  777.4 11.4 %collective-permute-done.62 = f32[256,128]{1,0:T(8,128)S(1)} collective-permute-done((f32[256,128]{1,0:T(8,128)S(1)}, f32[256,128]{1,0:T(8,128)S(1)}, u32[]{:S(2)}, u32[]{:S(2)}) %collective-permute-start.62) | collective-permute-done | bytes 131104 | tf_op jit(solution)/shard_map/ppermute | solution.py:12
  795.4 32.5 %collective-permute-done.63 = f32[256,128]{1,0:T(8,128)S(1)} collective-permute-done((f32[256,128]{1,0:T(8,128)S(1)}, f32[256,128]{1,0:T(8,128)S(1)}, u32[]{:S(2)}, u32[]{:S(2)}) %collective-permute-start.63) | collective-permute-done | bytes 131104 | tf_op jit(solution)/shard_map/ppermute | solution.py:12
  828.0 5.5 collective-permute-start.64
  836.8 6.5 collective-permute-start.65
  843.3 104.2 %all-reduce.9.cloned.1.call-done = f32[1280,128]{1,0:T(8,128)} async-done(((f32[1280,128]{1,0:T(8,128)}), f32[1280,128]{1,0:T(8,128)}) %all-reduce.9.cloned.1.call-update) | async-done | bytes 655376 | tf_op jit(solution)/shard_map/psum | solution.py:73
  947.4 6.2 fusion.20
  (219 shorter events, 218.6 us)
Async XLA Ops:
  7.2 293.2 %all-reduce.5.cloned.1.call-start = ((), (), s32[]{:S(2)}) async-start(), calls=%async_computation | async-start | bytes 1310720 | tf_op jit(solution)/shard_map/psum | solution.py:73
  7.2 15.7 %collective-permute-start.6 = (f32[256,128]{1,0:T(8,128)S(1)}, f32[256,128]{1,0:T(8,128)S(1)}, u32[]{:S(2)}, u32[]{:S(2)}) collective-permute-start(f32[256,128]{1,0:T(8,128)S(1)} %broadcast.294), channel_id=1, source_target_pairs={{0,8},{8,0},{16,24},{24,16},{32,40},{40,32},{48,56},{56,48},{64,72... | collective-permute-start | bytes 393224 | tf_op jit(solution)/shard_map/ppermute | solution.py:12
  29.5 13.9 %collective-permute-start.8 = (f32[256,128]{1,0:T(8,128)S(1)}, f32[256,128]{1,0:T(8,128)S(1)}, u32[]{:S(2)}, u32[]{:S(2)}) collective-permute-start(f32[256,128]{1,0:T(8,128)S(1)} %broadcast_select_fusion.37), channel_id=1, source_target_pairs={{0,32},{8,40},{16,48},{24,56},{32,0},{40,8},{48,16},{56,24},{64,96... | collective-permute-start | bytes 393224 | tf_op jit(solution)/shard_map/ppermute | solution.py:12
  32.3 13.9 %collective-permute-start.2 = (f32[256,128]{1,0:T(8,128)S(1)}, f32[256,128]{1,0:T(8,128)S(1)}, u32[]{:S(2)}, u32[]{:S(2)}) collective-permute-start(f32[256,128]{1,0:T(8,128)S(1)} %broadcast_select_fusion.38), channel_id=1, source_target_pairs={{0,32},{8,40},{16,48},{24,56},{32,0},{40,8},{48,16},{56,24},{64,96... | collective-permute-start | bytes 393224 | tf_op jit(solution)/shard_map/ppermute | solution.py:12
  43.4 25.5 %collective-permute-start.9 = (f32[256,128]{1,0:T(8,128)S(1)}, f32[256,128]{1,0:T(8,128)S(1)}, u32[]{:S(2)}, u32[]{:S(2)}) collective-permute-start(f32[256,128]{1,0:T(8,128)S(1)} %broadcast_select_fusion.40), channel_id=1, source_target_pairs={{0,64},{8,72},{16,80},{24,88},{32,96},{40,104},{48,112},{56,120},{... | collective-permute-start | bytes 393224 | tf_op jit(solution)/shard_map/ppermute | solution.py:12
  46.2 25.5 %collective-permute-start.3 = (f32[256,128]{1,0:T(8,128)S(1)}, f32[256,128]{1,0:T(8,128)S(1)}, u32[]{:S(2)}, u32[]{:S(2)}) collective-permute-start(f32[256,128]{1,0:T(8,128)S(1)} %broadcast_select_fusion.41), channel_id=1, source_target_pairs={{0,64},{8,72},{16,80},{24,88},{32,96},{40,104},{48,112},{56,120},{... | collective-permute-start | bytes 393224 | tf_op jit(solution)/shard_map/ppermute | solution.py:12
  75.3 11.6 %collective-permute-start.11 = (f32[256,128]{1,0:T(8,128)S(1)}, f32[256,128]{1,0:T(8,128)S(1)}, u32[]{:S(2)}, u32[]{:S(2)}) collective-permute-start(f32[256,128]{1,0:T(8,128)S(1)} %broadcast_select_fusion.46), channel_id=1, source_target_pairs={{0,256},{8,264},{16,272},{24,280},{32,288},{40,296},{48,304},{56,3... | collective-permute-start | bytes 393224 | tf_op jit(solution)/shard_map/ppermute | solution.py:12
  97.4 45.3 %collective-permute-start.13 = (f32[256,128]{1,0:T(8,128)S(1)}, f32[256,128]{1,0:T(8,128)S(1)}, u32[]{:S(2)}, u32[]{:S(2)}) collective-permute-start(f32[256,128]{1,0:T(8,128)S(1)} %broadcast_select_fusion.35), channel_id=1, source_target_pairs={{0,16},{8,24},{16,0},{24,8},{32,48},{40,56},{48,32},{56,40},{64,80... | collective-permute-start | bytes 393224 | tf_op jit(solution)/shard_map/ppermute | solution.py:12
  100.5 641.8 %all-reduce.7.cloned.1.call-start = ((), (), s32[]{:S(2)}) async-start(), calls=%async_computation.1 | async-start | bytes 1310720 | tf_op jit(solution)/shard_map/psum | solution.py:73
  142.7 19.9 %collective-permute-start.14 = (f32[256,128]{1,0:T(8,128)S(1)}, f32[256,128]{1,0:T(8,128)S(1)}, u32[]{:S(2)}, u32[]{:S(2)}) collective-permute-start(f32[256,128]{1,0:T(8,128)S(1)} %broadcast_select_fusion.36), channel_id=1, source_target_pairs={{0,32},{8,40},{16,48},{24,56},{32,0},{40,8},{48,16},{56,24},{64,96... | collective-permute-start | bytes 393224 | tf_op jit(solution)/shard_map/ppermute | solution.py:12
  162.7 146.4 %collective-permute-start.15 = (f32[256,128]{1,0:T(8,128)S(1)}, f32[256,128]{1,0:T(8,128)S(1)}, u32[]{:S(2)}, u32[]{:S(2)}) collective-permute-start(f32[256,128]{1,0:T(8,128)S(1)} %broadcast_select_fusion.39), channel_id=1, source_target_pairs={{0,64},{8,72},{16,80},{24,88},{32,96},{40,104},{48,112},{56,120},{... | collective-permute-start | bytes 393224 | tf_op jit(solution)/shard_map/ppermute | solution.py:12
  309.1 40.1 %collective-permute-start.16 = (f32[256,128]{1,0:T(8,128)S(1)}, f32[256,128]{1,0:T(8,128)S(1)}, u32[]{:S(2)}, u32[]{:S(2)}) collective-permute-start(f32[256,128]{1,0:T(8,128)S(1)} %broadcast_select_fusion.42), channel_id=1, source_target_pairs={{0,128},{8,136},{16,144},{24,152},{32,160},{40,168},{48,176},{56,1... | collective-permute-start | bytes 393224 | tf_op jit(solution)/shard_map/ppermute | solution.py:12
  342.3 11.4 %collective-permute-start.53 = (f32[128]{0:T(128)S(1)}, f32[128]{0:T(128)S(1)}, u32[]{:S(2)}, u32[]{:S(2)}) collective-permute-start(f32[128]{0:T(128)S(1)} %broadcast_select_fusion.60), channel_id=1, source_target_pairs={{0,256},{8,264},{16,272},{24,280},{32,288},{40,296},{48,304},{56,3... | collective-permute-start | bytes 1544 | tf_op jit(solution)/shard_map/ppermute | solution.py:12
  349.2 10.1 %collective-permute-start.17 = (f32[256,128]{1,0:T(8,128)S(1)}, f32[256,128]{1,0:T(8,128)S(1)}, u32[]{:S(2)}, u32[]{:S(2)}) collective-permute-start(f32[256,128]{1,0:T(8,128)S(1)} %broadcast_select_fusion.45), channel_id=1, source_target_pairs={{0,256},{8,264},{16,272},{24,280},{32,288},{40,296},{48,304},{56,3... | collective-permute-start | bytes 393224 | tf_op jit(solution)/shard_map/ppermute | solution.py:12
  353.8 9.7 %collective-permute-start.30 = (f32[256,128]{1,0:T(8,128)S(1)}, f32[256,128]{1,0:T(8,128)S(1)}, u32[]{:S(2)}, u32[]{:S(2)}) collective-permute-start(f32[256,128]{1,0:T(8,128)S(1)} %add.246), channel_id=1, source_target_pairs={{0,8},{8,0},{16,24},{24,16},{32,40},{40,32},{48,56},{56,48},{64,72... | collective-permute-start | bytes 393224 | tf_op jit(solution)/shard_map/ppermute | solution.py:12
  370.5 13.4 %collective-permute-start.32 = (f32[256,128]{1,0:T(8,128)S(1)}, f32[256,128]{1,0:T(8,128)S(1)}, u32[]{:S(2)}, u32[]{:S(2)}) collective-permute-start(f32[256,128]{1,0:T(8,128)S(1)} %broadcast_select_fusion.22), channel_id=1, source_target_pairs={{0,32},{8,40},{16,48},{24,56},{32,0},{40,8},{48,16},{56,24},{64,96... | collective-permute-start | bytes 393224 | tf_op jit(solution)/shard_map/ppermute | solution.py:12
  375.1 12.5 %collective-permute-start.20 = (f32[256,128]{1,0:T(8,128)S(1)}, f32[256,128]{1,0:T(8,128)S(1)}, u32[]{:S(2)}, u32[]{:S(2)}) collective-permute-start(f32[256,128]{1,0:T(8,128)S(1)} %broadcast_select_fusion.23), channel_id=1, source_target_pairs={{0,32},{8,40},{16,48},{24,56},{32,0},{40,8},{48,16},{56,24},{64,96... | collective-permute-start | bytes 393224 | tf_op jit(solution)/shard_map/ppermute | solution.py:12
  383.9 26.9 %collective-permute-start.33 = (f32[256,128]{1,0:T(8,128)S(1)}, f32[256,128]{1,0:T(8,128)S(1)}, u32[]{:S(2)}, u32[]{:S(2)}) collective-permute-start(f32[256,128]{1,0:T(8,128)S(1)} %broadcast_select_fusion.25), channel_id=1, source_target_pairs={{0,64},{8,72},{16,80},{24,88},{32,96},{40,104},{48,112},{56,120},{... | collective-permute-start | bytes 393224 | tf_op jit(solution)/shard_map/ppermute | solution.py:12
  387.7 26.0 %collective-permute-start.21 = (f32[256,128]{1,0:T(8,128)S(1)}, f32[256,128]{1,0:T(8,128)S(1)}, u32[]{:S(2)}, u32[]{:S(2)}) collective-permute-start(f32[256,128]{1,0:T(8,128)S(1)} %broadcast_select_fusion.26), channel_id=1, source_target_pairs={{0,64},{8,72},{16,80},{24,88},{32,96},{40,104},{48,112},{56,120},{... | collective-permute-start | bytes 393224 | tf_op jit(solution)/shard_map/ppermute | solution.py:12
  443.6 11.0 %collective-permute-start.38 = (f32[256,128]{1,0:T(8,128)S(1)}, f32[256,128]{1,0:T(8,128)S(1)}, u32[]{:S(2)}, u32[]{:S(2)}) collective-permute-start(f32[256,128]{1,0:T(8,128)S(1)} %broadcast_select_fusion.21), channel_id=1, source_target_pairs={{0,32},{8,40},{16,48},{24,56},{32,0},{40,8},{48,16},{56,24},{64,96... | collective-permute-start | bytes 393224 | tf_op jit(solution)/shard_map/ppermute | solution.py:12
  454.6 16.6 %collective-permute-start.39 = (f32[256,128]{1,0:T(8,128)S(1)}, f32[256,128]{1,0:T(8,128)S(1)}, u32[]{:S(2)}, u32[]{:S(2)}) collective-permute-start(f32[256,128]{1,0:T(8,128)S(1)} %broadcast_select_fusion.24), channel_id=1, source_target_pairs={{0,64},{8,72},{16,80},{24,88},{32,96},{40,104},{48,112},{56,120},{... | collective-permute-start | bytes 393224 | tf_op jit(solution)/shard_map/ppermute | solution.py:12
  496.2 13.8 %collective-permute-start.56 = (f32[256,128]{1,0:T(8,128)S(1)}, f32[256,128]{1,0:T(8,128)S(1)}, u32[]{:S(2)}, u32[]{:S(2)}) collective-permute-start(f32[256,128]{1,0:T(8,128)S(1)} %broadcast_select_fusion.6), channel_id=1, source_target_pairs={{0,32},{8,40},{16,48},{24,56},{32,0},{40,8},{48,16},{56,24},{64,96... | collective-permute-start | bytes 393224 | tf_op jit(solution)/shard_map/ppermute | solution.py:12
  499.0 13.8 %collective-permute-start.44 = (f32[256,128]{1,0:T(8,128)S(1)}, f32[256,128]{1,0:T(8,128)S(1)}, u32[]{:S(2)}, u32[]{:S(2)}) collective-permute-start(f32[256,128]{1,0:T(8,128)S(1)} %broadcast_select_fusion.7), channel_id=1, source_target_pairs={{0,32},{8,40},{16,48},{24,56},{32,0},{40,8},{48,16},{56,24},{64,96... | collective-permute-start | bytes 393224 | tf_op jit(solution)/shard_map/ppermute | solution.py:12
  510.0 23.9 %collective-permute-start.57 = (f32[256,128]{1,0:T(8,128)S(1)}, f32[256,128]{1,0:T(8,128)S(1)}, u32[]{:S(2)}, u32[]{:S(2)}) collective-permute-start(f32[256,128]{1,0:T(8,128)S(1)} %broadcast_select_fusion.9), channel_id=1, source_target_pairs={{0,64},{8,72},{16,80},{24,88},{32,96},{40,104},{48,112},{56,120},{... | collective-permute-start | bytes 393224 | tf_op jit(solution)/shard_map/ppermute | solution.py:12
  512.9 24.8 %collective-permute-start.45 = (f32[256,128]{1,0:T(8,128)S(1)}, f32[256,128]{1,0:T(8,128)S(1)}, u32[]{:S(2)}, u32[]{:S(2)}) collective-permute-start(f32[256,128]{1,0:T(8,128)S(1)} %broadcast_select_fusion.10), channel_id=1, source_target_pairs={{0,64},{8,72},{16,80},{24,88},{32,96},{40,104},{48,112},{56,120},{... | collective-permute-start | bytes 393224 | tf_op jit(solution)/shard_map/ppermute | solution.py:12
  549.4 398.1 %all-reduce.9.cloned.1.call-start = ((), (), s32[]{:S(2)}) async-start(), calls=%async_computation.2 | async-start | bytes 1310720 | tf_op jit(solution)/shard_map/psum | solution.py:73
  743.6 10.2 %collective-permute-start.66 = (f32[128]{0:T(128)S(1)}, f32[128]{0:T(128)S(1)}, u32[]{:S(2)}, u32[]{:S(2)}) collective-permute-start(f32[128]{0:T(128)S(1)} %get-tuple-element.6), channel_id=1, source_target_pairs={{0,8},{8,0},{16,24},{24,16},{32,40},{40,32},{48,56},{56,48},{64,72... | collective-permute-start | bytes 1544 | tf_op jit(solution)/shard_map/ppermute | solution.py:12
  772.1 16.7 %collective-permute-start.62 = (f32[256,128]{1,0:T(8,128)S(1)}, f32[256,128]{1,0:T(8,128)S(1)}, u32[]{:S(2)}, u32[]{:S(2)}) collective-permute-start(f32[256,128]{1,0:T(8,128)S(1)} %broadcast_select_fusion.5), channel_id=1, source_target_pairs={{0,32},{8,40},{16,48},{24,56},{32,0},{40,8},{48,16},{56,24},{64,96... | collective-permute-start | bytes 393224 | tf_op jit(solution)/shard_map/ppermute | solution.py:12
  774.0 16.7 %collective-permute-start.70 = (f32[128]{0:T(128)S(1)}, f32[128]{0:T(128)S(1)}, u32[]{:S(2)}, u32[]{:S(2)}) collective-permute-start(f32[128]{0:T(128)S(1)} %broadcast_select_fusion.53), channel_id=1, source_target_pairs={{0,128},{8,136},{16,144},{24,152},{32,160},{40,168},{48,176},{56,1... | collective-permute-start | bytes 1544 | tf_op jit(solution)/shard_map/ppermute | solution.py:12
  788.8 39.1 %collective-permute-start.63 = (f32[256,128]{1,0:T(8,128)S(1)}, f32[256,128]{1,0:T(8,128)S(1)}, u32[]{:S(2)}, u32[]{:S(2)}) collective-permute-start(f32[256,128]{1,0:T(8,128)S(1)} %broadcast_select_fusion.8), channel_id=1, source_target_pairs={{0,64},{8,72},{16,80},{24,88},{32,96},{40,104},{48,112},{56,120},{... | collective-permute-start | bytes 393224 | tf_op jit(solution)/shard_map/ppermute | solution.py:12
  790.8 42.7 %collective-permute-start.71 = (f32[128]{0:T(128)S(1)}, f32[128]{0:T(128)S(1)}, u32[]{:S(2)}, u32[]{:S(2)}) collective-permute-start(f32[128]{0:T(128)S(1)} %broadcast_select_fusion.54), channel_id=1, source_target_pairs={{0,256},{8,264},{16,272},{24,280},{32,288},{40,296},{48,304},{56,3... | collective-permute-start | bytes 1544 | tf_op jit(solution)/shard_map/ppermute | solution.py:12
  836.8 116.9 %collective-permute-start.65 = (f32[256,128]{1,0:T(8,128)S(1)}, f32[256,128]{1,0:T(8,128)S(1)}, u32[]{:S(2)}, u32[]{:S(2)}) collective-permute-start(f32[256,128]{1,0:T(8,128)S(1)} %broadcast_select_fusion.14), channel_id=1, source_target_pairs={{0,256},{8,264},{16,272},{24,280},{32,288},{40,296},{48,304},{56,3... | collective-permute-start | bytes 393224 | tf_op jit(solution)/shard_map/ppermute | solution.py:12
  (46 other events, 768.6 us)
Sparse Core Ops, SparseCore 0:
  100.6 199.6 all-reduce.4
  549.5 192.7 all-reduce.6
  758.3 189.1 all-reduce.8
where the time goes:
time: 964 us; the launch traced here: 962 us
  waiting for transfers between devices  582 us (60%)
  starting transfers between devices  237 us (25%)
  blocking collectives  80.1 us (8%)
  other arithmetic  29.7 us (3%)
  between operations  23.5 us (2%)
    psum x3, waiting for transfers between devices, per_device(): user_stat, beta_total = lax.psum((user_local, beta_cols), 'items')  392 us
    ppermute x72, starting transfers between devices, swapped(): return lax.ppermute(value, axis, pairs)  236 us
    ppermute x72, waiting for transfers between devices, swapped(): return lax.ppermute(value, axis, pairs)  189 us
    psum x2, blocking collectives, per_device(): user_stat, beta_total = lax.psum((user_local, beta_cols), 'items')  80.1 us
  transfers between devices with their start and end apart: 75, of which 38 were waited for; matrix products, arithmetic and copies ran while one was open for 3% of the time, Pallas kernels for 0%

commit v1 on v0

v1 whole, which is shorter than its diff:
```python
import functools

import jax
import jax.numpy as jnp
from jax import lax
from jax.experimental import pallas as pl
from jax.experimental.pallas import tpu as pltpu
from jax.sharding import PartitionSpec as P

MESH = pl.DeviceIdType.MESH
STRATA = 3
UNITS = 128
USERS = 1280
ITEMS = 256
QUARTER = 320
SENT = QUARTER + 8
ROUTED = ITEMS + 8
FACTOR = 64.0
CORE, Z0, Z1, Z2, Y0, Y1 = 1, 2, 4, 8, 16, 32
HOME = 63
ORDER = (Z2, Z1, Z0, Y1, Y0, CORE)


def cotangent(x):
    r = x - jnp.floor(x + 0.5)
    s = r * r
    series = 1.2898681 + s * (
        0.16464647 + s * (0.034686124 + s * (0.0081547124 + s * (0.0019891502 + s * 0.00049217311)))
    )
    return (1.0 - 3.0 * s) / (r * (1.0 - s)) - r * series


def digamma_parts(x, positive=False):
    if positive:
        z = x
    else:
        negative = x <= 0.0
        z = jnp.where(negative, 1.0 - x, x)
    y = z + 4.0
    inverse = 1.0 / y
    square = inverse * inverse
    tail = 0.5 * inverse + square * (
        0.083333333 - square * (0.0083333333 - square * 0.003968254)
    )
    low = jnp.minimum(z, 1e8)
    p = low * (low + 3.0)
    e = -tail - (2.0 * low + 3.0) * (2.0 * p + 2.0) / (p * (p + 2.0))
    if not positive:
        e = jnp.where(negative, e - cotangent(x), e)
    return y, e


def inverse_rate(rte):
    return jnp.where(rte >= 0.0, 1.0 / rte, jnp.nan)


def exp_log(shp, rte, positive=False):
    y, e = digamma_parts(shp, positive)
    return y * inverse_rate(rte) * jnp.exp(e)


def log_mean(shp, rte):
    y, e = digamma_parts(shp)
    return jnp.log(y) + e - jnp.log(rte)


def rows8(row):
    return jnp.broadcast_to(row, (8, UNITS))


def column_sum(value):
    return jnp.sum(value, axis=0, keepdims=True)


def kernel(
    match_ref, inter_hbm, user_ref, item_ref, ulog_ref, ilog_ref,
    inter, route_src, route_dst, rs_src, rs_dst, zh_src, zh_dst, ag_src, ag_dst, fin_src, fin_dst,
    visit, uexp, iexp, istat, ushp,
    load_sem, route_ss, route_rs, rs_ss, rs_rs, zh_ss, zh_rs, ag_ss, ag_rs, fin_ss, fin_rs,
):
    u = lax.axis_index("users")
    i = lax.axis_index("items")
    x = i // 2

    def at_user(mask):
        return (u ^ mask, i)

    def at_x(step):
        return (u, (i + 2 * step) % 8)

    at_zh = (u, i ^ 1)

    loads = [
        pltpu.make_async_copy(inter_hbm.at[s], inter.at[s], load_sem.at[s]) for s in range(STRATA)
    ]
    for load in loads:
        load.start()

    barrier = pltpu.get_barrier_semaphore()
    partners = [at_user(mask) for mask in ORDER + (HOME,)] + [at_x(1), at_x(2), at_x(3), at_zh]
    for partner in partners:
        pl.semaphore_signal(barrier, inc=1, device_id=partner, device_id_type=MESH)

    def remote(src, dst, ss, rs, device):
        return pltpu.make_async_remote_copy(
            src_ref=src, dst_ref=dst, send_sem=ss, recv_sem=rs, device_id=device, device_id_type=MESH
        )

    def route_copy(s, stage):
        return remote(
            route_src.at[s, stage], route_dst.at[s, stage], route_ss.at[s, stage],
            route_rs.at[s, stage], at_user(ORDER[stage]),
        )

    def rs_copy(s, step):
        return remote(
            rs_src.at[s, step], rs_dst.at[s, step - 1], rs_ss.at[s, step - 1],
            rs_rs.at[s, step - 1], at_x(step),
        )

    def zh_copy(s):
        return remote(zh_src.at[s], zh_dst.at[s], zh_ss.at[s], zh_rs.at[s], at_zh)

    def ag_copy(s, step):
        return remote(
            ag_src.at[s], ag_dst.at[s, step - 1], ag_ss.at[s, step - 1], ag_rs.at[s, step - 1],
            at_x(step),
        )

    m0, m1 = match_ref[0], match_ref[1]
    routes = (m0, m0 ^ m1, m1 ^ HOME)

    def route_next(s, stage):
        route_copy(s, stage).wait_recv()
        picked = (routes[s] & ORDER[stage]) != 0
        value = jnp.where(picked, route_dst[s, stage], route_src[s, stage])
        if stage + 1 < len(ORDER):
            route_src[s, stage + 1] = value
            route_copy(s, stage + 1).start()
        else:
            visit[...] = value

    route_src[0, 0, 0:ITEMS] = item_ref[...].astype(jnp.float32)
    route_src[0, 0, ITEMS:] = jnp.ones((8, UNITS), jnp.float32)

    pl.semaphore_wait(barrier, len(partners))
    route_copy(0, 0).start()

    def first_users(d, total):
        rows = pl.ds(((x + d) % 4) * QUARTER, QUARTER)
        shp = user_ref[rows, :].astype(jnp.float32)
        uexp[d] = exp_log(shp, jnp.ones((1, UNITS), jnp.float32), True).astype(jnp.bfloat16)
        return total + column_sum(shp)

    theta = lax.fori_loop(0, 4, first_users, jnp.zeros((1, UNITS), jnp.float32))
    ushp[...] = user_ref[pl.ds(x * QUARTER, QUARTER), :].astype(jnp.float32)
    urte = jnp.ones((1, UNITS), jnp.float32)

    for stage in range(len(ORDER)):
        route_next(0, stage)

    for s in range(STRATA):
        shp = visit[0:ITEMS]
        rte = visit[ITEMS : ITEMS + 1]
        iexp[...] = exp_log(shp, rte).astype(jnp.bfloat16)
        beta = rows8(column_sum(shp) / rte)
        istat[...] = jnp.zeros_like(istat)
        loads[s].wait()

        def users_of(d):
            rows = pl.ds(((x + d) % 4) * QUARTER, QUARTER)
            ue = uexp[d]
            ie = iexp[...]
            denominator = lax.dot_general(
                ue, ie, (((1,), (1,)), ((), ())), preferred_element_type=jnp.float32
            )
            ratios = (inter[s, rows, :].astype(jnp.float32) / denominator).astype(jnp.bfloat16)
            rs_src[s, d, 0:QUARTER] = ue.astype(jnp.float32) * jnp.dot(
                ratios, ie, preferred_element_type=jnp.float32
            )
            rs_src[s, d, QUARTER:] = beta
            istat[...] += lax.dot_general(
                ratios, ue, (((0,), (0,)), ((), ())), preferred_element_type=jnp.float32
            )

        def users_sent(d, carry):
            users_of(d)
            rs_copy(s, d).start()
            return carry

        lax.fori_loop(1, 4, users_sent, 0)
        users_of(0)

        new_shp = 0.5 * shp + 0.5 * (0.3 + FACTOR * (iexp[...].astype(jnp.float32) * istat[...]))
        new_rte = 0.5 * rte + 0.5 * (0.3 + FACTOR * theta)
        last = s == STRATA - 1
        if last:
            fin_src[...] = log_mean(new_shp, new_rte)
            final = remote(fin_src, fin_dst, fin_ss, fin_rs, at_user(HOME))
            final.start()
        else:
            route_src[s + 1, 0, 0:ITEMS] = new_shp
            route_src[s + 1, 0, ITEMS:] = rows8(new_rte)
            route_copy(s + 1, 0).start()

        for step in range(1, 4):
            rs_copy(s, step).wait_recv()
        zh_src[s] = (rs_src[s, 0] + rs_dst[s, 0]) + (rs_dst[s, 1] + rs_dst[s, 2])
        zh_copy(s).start()

        if not last:
            route_next(s + 1, 0)
            route_next(s + 1, 1)

        zh_copy(s).wait_recv()
        total = zh_src[s] + zh_dst[s]
        urte = 0.5 * urte + 0.5 * (0.3 + FACTOR * total[QUARTER : QUARTER + 1])
        own = 0.5 * ushp[...] + 0.5 * (0.3 + FACTOR * total[0:QUARTER])
        ushp[...] = own
        if last:
            result = log_mean(own, urte)
            ag_src[s, 0:QUARTER] = result
            ag_src[s, QUARTER:] = jnp.zeros((8, UNITS), jnp.float32)
        else:
            result = exp_log(own, urte)
            ag_src[s, 0:QUARTER] = result
            ag_src[s, QUARTER:] = rows8(column_sum(own) / urte)
        for step in range(1, 4):
            ag_copy(s, step).start()

        if last:
            final.wait_recv()
            ilog_ref[...] = fin_dst[...].astype(jnp.bfloat16)
            ulog_ref[pl.ds(x * QUARTER, QUARTER), :] = result.astype(jnp.bfloat16)
            for step in range(1, 4):
                ag_copy(s, step).wait_recv()
                rows = pl.ds(((x + 4 - step) % 4) * QUARTER, QUARTER)
                ulog_ref[rows, :] = ag_dst[s, step - 1, 0:QUARTER].astype(jnp.bfloat16)
        else:
            uexp[0] = result.astype(jnp.bfloat16)
            route_next(s + 1, 2)
            route_next(s + 1, 3)
            theta = ag_src[s, QUARTER : QUARTER + 1]
            for step in range(1, 4):
                ag_copy(s, step).wait_recv()
                uexp[4 - step] = ag_dst[s, step - 1, 0:QUARTER].astype(jnp.bfloat16)
                theta = theta + ag_dst[s, step - 1, QUARTER : QUARTER + 1]
            route_next(s + 1, 4)
            route_next(s + 1, 5)

    for s in range(STRATA):
        for stage in range(len(ORDER)):
            route_copy(s, stage).wait_send()
        for step in range(1, 4):
            rs_copy(s, step).wait_send()
            ag_copy(s, step).wait_send()
        zh_copy(s).wait_send()
    final.wait_send()


def per_device(interactions, matchings, user_shape, item_shape):
    stages = len(ORDER)
    f32, dma = jnp.float32, pltpu.SemaphoreType.DMA
    vmem = pl.BlockSpec(memory_space=pltpu.VMEM)
    return pl.pallas_call(
        kernel,
        out_shape=(
            jax.ShapeDtypeStruct((USERS, UNITS), jnp.bfloat16),
            jax.ShapeDtypeStruct((ITEMS, UNITS), jnp.bfloat16),
        ),
        in_specs=[
            pl.BlockSpec(memory_space=pltpu.SMEM),
            pl.BlockSpec(memory_space=pl.ANY),
            vmem,
            vmem,
        ],
        out_specs=(vmem, vmem),
        scratch_shapes=[
            pltpu.VMEM((STRATA, USERS, ITEMS), jnp.bfloat16),
            pltpu.VMEM((STRATA, stages, ROUTED, UNITS), f32),
            pltpu.VMEM((STRATA, stages, ROUTED, UNITS), f32),
            pltpu.VMEM((STRATA, 4, SENT, UNITS), f32),
            pltpu.VMEM((STRATA, 3, SENT, UNITS), f32),
            pltpu.VMEM((STRATA, SENT, UNITS), f32),
            pltpu.VMEM((STRATA, SENT, UNITS), f32),
            pltpu.VMEM((STRATA, SENT, UNITS), f32),
            pltpu.VMEM((STRATA, 3, SENT, UNITS), f32),
            pltpu.VMEM((ITEMS, UNITS), f32),
            pltpu.VMEM((ITEMS, UNITS), f32),
            pltpu.VMEM((ROUTED, UNITS), f32),
            pltpu.VMEM((4, QUARTER, UNITS), jnp.bfloat16),
            pltpu.VMEM((ITEMS, UNITS), jnp.bfloat16),
            pltpu.VMEM((ITEMS, UNITS), f32),
            pltpu.VMEM((QUARTER, UNITS), f32),
            dma((STRATA,)),
            dma((STRATA, stages)),
            dma((STRATA, stages)),
            dma((STRATA, 3)),
            dma((STRATA, 3)),
            dma((STRATA,)),
            dma((STRATA,)),
            dma((STRATA, 3)),
            dma((STRATA, 3)),
            dma,
            dma,
        ],
        compiler_params=pltpu.CompilerParams(
            collective_id=0, has_side_effects=True, vmem_limit_bytes=40 << 20
        ),
        cost_estimate=pl.CostEstimate(
            flops=3 * 6 * USERS * ITEMS * UNITS, bytes_accessed=3 << 20, transcendentals=1 << 20
        ),
    )(matchings, interactions, user_shape, item_shape)


def solution(mesh):
    placed = (P(None, "users", "items"), P(), P("users", None), P(("users", "items"), None))
    return jax.shard_map(
        per_device,
        mesh=mesh,
        in_specs=placed,
        out_specs=(P("users", None), P(("users", "items"), None)),
        check_vma=False,
    )
```

time: 964 us -> 197 us (0.20)
  the two profiles are of different devices: /device:TPU:1 before, /device:TPU:56 now
where the time goes in v1:
time: 197 us
  Pallas kernels  191 us (97%)
  local copies, waits for them, and re-layouts  5.36 us (3%)
    pallas_call x1, Pallas kernels, per_device(): pl.pallas_call(kernel, out_shape=(jax.ShapeDtypeStruct((USERS, UNITS), jn...  191 us
    unnamed x10, local copies, waits for them, and re-layouts  5.36 us

profile of v1, /device:TPU:56, one launch (start us, length us, event | category | flops | bytes accessed | tf_op | source)
XLA Modules:
  0.0 196.7 jit_solution(15960386709983305399)
XLA Ops:
  0.6 0.0 copy-start
  0.6 1.5 copy-done
  2.2 0.0 copy-start.1
  2.2 1.0 copy-done.1
  3.1 0.0 copy-start.2
  3.2 0.8 copy-done.2
  4.0 0.0 copy-start.3
  4.0 0.7 copy-done.3
  4.6 190.6 %shard_map.59 = (bf16[1280,128]{1,0:T(8,128)(2,1)S(1)}, bf16[256,128]{1,0:T(8,128)(2,1)S(1)}) custom-call(s32[3]{0:T(128)S(1)} %copy-done.3, bf16[3,1280,256]{2,1,0:T(8,128)(2,1)S(1)} %copy-done, bf16[1280,128]{1,0:T(8,128)(2,1)S(1)} %copy-done.1, bf16[256,128]{1,0:T(8,128)(2,1)S(1)} %copy-done.2), custom_call_target="tpu_custom_call" | custom-call | flops 754974720 | bytes 3145728 | tf_op jit(solution)/shard_map/pallas_call | solution.py:265
  195.3 0.7 copy.8
  196.0 0.6 copy.9
Async XLA Ops:
  0.6 1.5 copy-start
  2.2 1.0 copy-start.1
  3.1 0.8 copy-start.2
  4.0 0.7 copy-start.3

commit v2 on v1

v2 whole, which is shorter than its diff:
```python
import functools

import jax
import jax.numpy as jnp
from jax import lax
from jax.experimental import pallas as pl
from jax.experimental.pallas import tpu as pltpu
from jax.sharding import PartitionSpec as P

MESH = pl.DeviceIdType.MESH
STRATA = 3
UNITS = 128
USERS = 1280
ITEMS = 256
QUARTER = 320
PIECES = 4
PIECE = QUARTER // PIECES
SENT = QUARTER + 8
ROUTED = ITEMS + 8
FACTOR = 64.0
CORE, Z0, Z1, Z2, Y0, Y1 = 1, 2, 4, 8, 16, 32
HOME = 63
MASKS = (CORE, Z0, Z1, Y0, Y1)
STAGES = len(MASKS) + 1
FAR = Z2
PARTS = (
    (0, 128, (FAR, Z1, Z0, Y1, Y0, CORE)),
    (128, 136, (Y1, Y0, CORE, FAR, Z1, Z0)),
)
STAGE_TIME = {CORE: 1.0, Z0: 2.9, Z1: 3.5, FAR: 7.0, Y0: 2.9, Y1: 3.5}
SCATTERED, SCATTER_STEP, EXCHANGED, EXCHANGE_STEP = 3.0, 1.7, 11.0, 3.5


def cotangent(x):
    r = x - jnp.floor(x + 0.5)
    s = r * r
    series = 1.2898681 + s * (
        0.16464647 + s * (0.034686124 + s * (0.0081547124 + s * (0.0019891502 + s * 0.00049217311)))
    )
    return (1.0 - 3.0 * s) / (r * (1.0 - s)) - r * series


def digamma_parts(x, positive=False):
    if positive:
        z = x
    else:
        negative = x <= 0.0
        z = jnp.where(negative, 1.0 - x, x)
    y = z + 4.0
    inverse = 1.0 / y
    square = inverse * inverse
    tail = 0.5 * inverse + square * (
        0.083333333 - square * (0.0083333333 - square * 0.003968254)
    )
    low = jnp.minimum(z, 1e8)
    p = low * (low + 3.0)
    e = -tail - (2.0 * low + 3.0) * (2.0 * p + 2.0) / (p * (p + 2.0))
    if not positive:
        e = jnp.where(negative, e - cotangent(x), e)
    return y, e


def inverse_rate(rte):
    return jnp.where(rte >= 0.0, 1.0 / rte, jnp.nan)


def exp_log(shp, rte, positive=False):
    y, e = digamma_parts(shp, positive)
    return y * inverse_rate(rte) * jnp.exp(e)


def log_mean(shp, rte):
    y, e = digamma_parts(shp)
    return jnp.log(y) + e - jnp.log(rte)


def in_rows(count, step, body):
    def once(n, carry):
        body(pl.ds(pl.multiple_of(n * step, step), step))
        return carry

    lax.fori_loop(0, count // step, once, 0)


def rows8(row):
    return jnp.broadcast_to(row, (8, UNITS))


def column_sum(value):
    return jnp.sum(value, axis=0, keepdims=True)


def kernel(
    far, match_hbm, inter_hbm, user_hbm, item_hbm, ulog_ref, ilog_ref,
    match_ref, inter, user_ref, item_ref,
    route_src, route_dst, rs_src, rs_dst, zh_src, zh_dst, ag_src, ag_dst, fin_src, fin_dst,
    visit, uexp, iexp, istat, ushp,
    load_sem, route_ss, route_rs, rs_ss, rs_rs, zh_ss, zh_rs, ag_ss, ag_rs, fin_ss, fin_rs,
):
    u = lax.axis_index("users")
    i = lax.axis_index("items")
    x = i // 2

    def at_user(mask):
        return (u ^ mask, i)

    def at_x(step):
        return (u, (i + 2 * step) % 8)

    at_zh = (u, i ^ 1)

    barrier = pltpu.get_barrier_semaphore()
    moves = MASKS + (HOME,) + tuple(sorted(set(far) - {0}))
    partners = [at_user(mask) for mask in moves] + [at_x(1), at_x(2), at_x(3), at_zh]
    for partner in partners:
        pl.semaphore_signal(barrier, inc=1, device_id=partner, device_id_type=MESH)

    load_item = pltpu.make_async_copy(item_hbm, item_ref, load_sem.at[STRATA])
    load_user = pltpu.make_async_copy(user_hbm, user_ref, load_sem.at[STRATA + 1])
    load_match = pltpu.make_async_copy(match_hbm, match_ref, load_sem.at[STRATA + 2])
    loads = [
        pltpu.make_async_copy(inter_hbm.at[s], inter.at[s], load_sem.at[s]) for s in range(STRATA)
    ]
    for load in [load_item, load_match, load_user] + loads:
        load.start()

    def remote(src, dst, ss, rs, device):
        return pltpu.make_async_remote_copy(
            src_ref=src, dst_ref=dst, send_sem=ss, recv_sem=rs, device_id=device, device_id_type=MESH
        )

    def route_part(s, part):
        first, rows, order = PARTS[part]
        masks = tuple(far[s] if mask == FAR else mask for mask in order)
        return first, rows, tuple(mask for mask in masks if mask)

    def route_copy(s, part, stage):
        first, rows, order = route_part(s, part)
        rows = pl.ds(first, rows)
        return remote(
            route_src.at[s, stage, rows], route_dst.at[s, stage, rows], route_ss.at[s],
            route_rs.at[s, part, stage], at_user(order[stage]),
        )

    def rs_rows(piece):
        return pl.ds(8 + piece * PIECE, PIECE) if piece else pl.ds(0, 8 + PIECE)

    def rs_copy(s, step, piece):
        rows = rs_rows(piece)
        return remote(
            rs_src.at[s, step, rows], rs_dst.at[s, step - 1, rows], rs_ss.at[s],
            rs_rs.at[s, piece], at_x(step),
        )

    def zh_copy(s, piece):
        rows = rs_rows(piece)
        return remote(
            zh_src.at[s, rows], zh_dst.at[s, rows], zh_ss.at[s], zh_rs.at[s, piece], at_zh
        )

    def ag_copy(s, step, piece):
        more = 8 if piece == PIECES - 1 else 0
        rows = pl.ds(piece * PIECE, PIECE + more)
        return remote(
            ag_src.at[s, rows], ag_dst.at[s, step - 1, rows], ag_ss.at[s], ag_rs.at[s], at_x(step),
        )

    def wait_bytes(ref, sem):
        pltpu.make_async_copy(ref, ref, sem).wait()

    def routed(s):
        events = []
        for part in range(len(PARTS)):
            at = 0.0
            for stage, mask in enumerate(route_part(s, part)[2]):
                at += STAGE_TIME[mask]
                events.append((at, functools.partial(route_next, s, part, stage)))
        return events

    def run(events):
        for _, event in sorted(events, key=lambda timed: timed[0]):
            event()

    def route_next(s, part, stage):
        first, rows, order = route_part(s, part)
        rows = pl.ds(first, rows)
        route_copy(s, part, stage).wait_recv()
        if order[stage] & FAR:
            value = route_dst[s, stage, rows]
        else:
            m0, m1 = match_ref[0], match_ref[1]
            mask = (m0, m0 ^ m1, m1 ^ HOME)[s]
            picked = (mask & order[stage]) != 0
            value = jnp.where(picked, route_dst[s, stage, rows], route_src[s, stage, rows])
        if stage + 1 < len(order):
            route_src[s, stage + 1, rows] = value
            route_copy(s, part, stage + 1).start()
        else:
            visit[rows] = value

    load_item.wait()
    route_src[0, 0, 0:ITEMS] = item_ref[...].astype(jnp.float32)
    route_src[0, 0, ITEMS:] = jnp.ones((8, UNITS), jnp.float32)
    load_match.wait()
    load_user.wait()

    pl.semaphore_wait(barrier, len(partners))
    for part in range(len(PARTS)):
        route_copy(0, part, 0).start()

    def first_users(d, total):
        rows = pl.ds(((x + d) % 4) * QUARTER, QUARTER)
        shp = user_ref[rows, :].astype(jnp.float32)
        uexp[d] = exp_log(shp, jnp.ones((1, UNITS), jnp.float32), True).astype(jnp.bfloat16)
        return total + column_sum(shp)

    theta = lax.fori_loop(0, 4, first_users, jnp.zeros((1, UNITS), jnp.float32))
    ushp[...] = user_ref[pl.ds(x * QUARTER, QUARTER), :].astype(jnp.float32)
    urte = jnp.ones((1, UNITS), jnp.float32)

    run(routed(0))

    for s in range(STRATA):
        last = s == STRATA - 1
        rte = visit[ITEMS : ITEMS + 1]

        def item_rows(rows):
            iexp[rows] = exp_log(visit[rows], rte).astype(jnp.bfloat16)

        in_rows(ITEMS, 64, item_rows)
        rs_src[s, :, 0:8] = jnp.broadcast_to(column_sum(visit[0:ITEMS]) / rte, (4, 8, UNITS))
        istat[...] = jnp.zeros_like(istat)
        loads[s].wait()

        def users_of(d, first, rows):
            weights = inter[s, pl.ds(((x + d) % 4) * QUARTER + first, rows), :]
            ue = uexp[d, first : first + rows]
            ie = iexp[...]
            denominator = lax.dot_general(
                ue, ie, (((1,), (1,)), ((), ())), preferred_element_type=jnp.float32
            )
            ratios = (weights.astype(jnp.float32) / denominator).astype(jnp.bfloat16)
            rs_src[s, d, 8 + first : 8 + first + rows] = ue.astype(jnp.float32) * jnp.dot(
                ratios, ie, preferred_element_type=jnp.float32
            )
            istat[...] += lax.dot_general(
                ratios, ue, (((0,), (0,)), ((), ())), preferred_element_type=jnp.float32
            )

        for half in range(2):
            def users_sent(n, carry, half=half):
                d = (n + 1) % 4
                users_of(d, half * (QUARTER // 2), QUARTER // 2)

                @pl.when(n < 3)
                def _():
                    for piece in range(half * PIECES // 2, (half + 1) * PIECES // 2):
                        rs_copy(s, n + 1, piece).start()

                return carry

            lax.fori_loop(0, 4, users_sent, 0)

        new_rte = 0.5 * rte + 0.5 * (0.3 + FACTOR * theta)

        def new_rows(rows):
            stat = iexp[rows].astype(jnp.float32) * istat[rows]
            shp = 0.5 * visit[rows] + 0.5 * (0.3 + FACTOR * stat)
            if last:
                fin_src[rows] = log_mean(shp, new_rte)
            else:
                route_src[s + 1, 0, rows] = shp

        in_rows(ITEMS, 64, new_rows)
        if last:
            final = remote(fin_src, fin_dst, fin_ss, fin_rs, at_user(HOME))
            final.start()
        else:
            route_src[s + 1, 0, ITEMS:] = rows8(new_rte)
            for part in range(len(PARTS)):
                route_copy(s + 1, part, 0).start()

        state = {"urte": urte, "columns": jnp.zeros((1, UNITS), jnp.float32)}

        def scattered(piece):
            rows = rs_rows(piece)
            wait_bytes(rs_dst.at[s, :, rows], rs_rs.at[s, piece])
            zh_src[s, rows] = (rs_src[s, 0, rows] + rs_dst[s, 0, rows]) + (
                rs_dst[s, 1, rows] + rs_dst[s, 2, rows]
            )
            zh_copy(s, piece).start()

        def exchanged(piece):
            zh_copy(s, piece).wait_recv()
            if piece == 0:
                beta = zh_src[s, 0:1] + zh_dst[s, 0:1]
                state["urte"] = 0.5 * state["urte"] + 0.5 * (0.3 + FACTOR * beta)
            mine = pl.ds(piece * PIECE, PIECE)
            stat = pl.ds(8 + piece * PIECE, PIECE)
            own = 0.5 * ushp[mine] + 0.5 * (0.3 + FACTOR * (zh_src[s, stat] + zh_dst[s, stat]))
            ushp[mine] = own
            if last:
                ag_src[s, mine] = log_mean(own, state["urte"])
            else:
                ag_src[s, mine] = exp_log(own, state["urte"])
                state["columns"] += column_sum(own)
            if piece == PIECES - 1:
                ag_src[s, QUARTER:] = rows8(state["columns"] / state["urte"])
            for step in range(1, 4):
                ag_copy(s, step, piece).start()

        events = [] if last else routed(s + 1)
        for piece in range(PIECES):
            events.append((SCATTERED + piece * SCATTER_STEP, functools.partial(scattered, piece)))
            events.append((EXCHANGED + piece * EXCHANGE_STEP, functools.partial(exchanged, piece)))
        run(events)
        urte = state["urte"]

        if last:
            final.wait_recv()
            ilog_ref[...] = fin_dst[...].astype(jnp.bfloat16)
            ulog_ref[pl.ds(x * QUARTER, QUARTER), :] = ag_src[s, 0:QUARTER].astype(jnp.bfloat16)
        else:
            uexp[0] = ag_src[s, 0:QUARTER].astype(jnp.bfloat16)
            theta = ag_src[s, QUARTER : QUARTER + 1]
        wait_bytes(ag_dst.at[s], ag_rs.at[s])
        for step in range(1, 4):
            value = ag_dst[s, step - 1, 0:QUARTER].astype(jnp.bfloat16)
            if last:
                ulog_ref[pl.ds(((x + 4 - step) % 4) * QUARTER, QUARTER), :] = value
            else:
                uexp[4 - step] = value
                theta = theta + ag_dst[s, step - 1, QUARTER : QUARTER + 1]

    for s in range(STRATA):
        wait_bytes(route_src.at[s, 0 : len(route_part(s, 0)[2])], route_ss.at[s])
        wait_bytes(rs_src.at[s, 1:4], rs_ss.at[s])
        wait_bytes(zh_src.at[s], zh_ss.at[s])
        wait_bytes(ag_dst.at[s], ag_ss.at[s])
    final.wait_send()


def call(far, number, interactions, matchings, user_shape, item_shape):
    f32, dma = jnp.float32, pltpu.SemaphoreType.DMA
    vmem = pl.BlockSpec(memory_space=pltpu.VMEM)
    hbm = pl.BlockSpec(memory_space=pltpu.HBM)
    return pl.pallas_call(
        functools.partial(kernel, far),
        out_shape=(
            jax.ShapeDtypeStruct((USERS, UNITS), jnp.bfloat16),
            jax.ShapeDtypeStruct((ITEMS, UNITS), jnp.bfloat16),
        ),
        in_specs=[hbm, hbm, hbm, hbm],
        out_specs=(vmem, vmem),
        scratch_shapes=[
            pltpu.SMEM((STRATA,), jnp.int32),
            pltpu.VMEM((STRATA, USERS, ITEMS), jnp.bfloat16),
            pltpu.VMEM((USERS, UNITS), jnp.bfloat16),
            pltpu.VMEM((ITEMS, UNITS), jnp.bfloat16),
            pltpu.VMEM((STRATA, STAGES, ROUTED, UNITS), f32),
            pltpu.VMEM((STRATA, STAGES, ROUTED, UNITS), f32),
            pltpu.VMEM((STRATA, 4, SENT, UNITS), f32),
            pltpu.VMEM((STRATA, 3, SENT, UNITS), f32),
            pltpu.VMEM((STRATA, SENT, UNITS), f32),
            pltpu.VMEM((STRATA, SENT, UNITS), f32),
            pltpu.VMEM((STRATA, SENT, UNITS), f32),
            pltpu.VMEM((STRATA, 3, SENT, UNITS), f32),
            pltpu.VMEM((ITEMS, UNITS), f32),
            pltpu.VMEM((ITEMS, UNITS), f32),
            pltpu.VMEM((ROUTED, UNITS), f32),
            pltpu.VMEM((4, QUARTER, UNITS), jnp.bfloat16),
            pltpu.VMEM((ITEMS, UNITS), jnp.bfloat16),
            pltpu.VMEM((ITEMS, UNITS), f32),
            pltpu.VMEM((QUARTER, UNITS), f32),
            dma((STRATA + 3,)),
            dma((STRATA,)),
            dma((STRATA, len(PARTS), STAGES)),
            dma((STRATA,)),
            dma((STRATA, PIECES)),
            dma((STRATA,)),
            dma((STRATA, PIECES)),
            dma((STRATA,)),
            dma((STRATA,)),
            dma,
            dma,
        ],
        compiler_params=pltpu.CompilerParams(
            collective_id=number, has_side_effects=True, vmem_limit_bytes=63 << 20
        ),
        cost_estimate=pl.CostEstimate(
            flops=3 * 6 * USERS * ITEMS * UNITS, bytes_accessed=3 << 20, transcendentals=1 << 20
        ),
    )(matchings, interactions, user_shape, item_shape)


def per_device(interactions, matchings, user_shape, item_shape):
    calls = []
    for first in range(2):
        for second in range(2):
            far = (first * FAR, (first ^ second) * FAR, (second ^ 1) * FAR)
            calls.append(functools.partial(call, far, len(calls)))
    bits = (matchings // FAR) & 1
    return lax.switch(
        bits[0] * 2 + bits[1], calls, interactions, matchings, user_shape, item_shape
    )


def solution(mesh):
    placed = (P(None, "users", "items"), P(), P("users", None), P(("users", "items"), None))
    return jax.shard_map(
        per_device,
        mesh=mesh,
        in_specs=placed,
        out_specs=(P("users", None), P(("users", "items"), None)),
        check_vma=False,
    )
```

time: 197 us -> 181 us (0.919)
  the two profiles are of different devices: /device:TPU:56 before, /device:TPU:104 now
where the time goes in v2:
time: 181 us; the launch traced here: 180 us
  Pallas kernels  175 us (97%)
  local copies, waits for them, and re-layouts  1.94 us (1%)
  between operations  1.94 us (1%)
    pallas_call x1, Pallas kernels, call(): pl.pallas_call(functools.partial(kernel, far), out_shape=(jax.ShapeDtypeS...  175 us

profile of v2, /device:TPU:104, one launch (start us, length us, event | category | flops | bytes accessed | tf_op | source)
XLA Modules:
  0.0 180.4 jit_solution(7675710000258117729)
XLA Ops:
  0.6 0.7 fusion
  1.3 0.6 fusion.1
  3.2 175.9 %conditional.1 = ((bf16[1280,128]{1,0:T(8,128)(2,1)S(1)}, bf16[256,128]{1,0:T(8,128)(2,1)S(1)})) conditional(s32[]{:T(128)} %bitcast, (s32[3]{0:T(128)}, bf16[3,1280,256]{2,1,0:T(8,128)(2,1)}, bf16[1280,128]{1,0:T(8,128)(2,1)}, bf16[256,128]{1,0:T(8,128)(2,1)}) %tuple.19, (s32[3]{0:T(128)}, ...), branch_computations={%region_0.1_spmd, %region_1.2_spmd, %region_2.3_spmd, %region_3.4_... | conditional | flops 754974720 | bytes 3145736 | solution.py:403
  3.4 175.5 %branch_2_fun.1 = (bf16[1280,128]{1,0:T(8,128)(2,1)S(1)}, bf16[256,128]{1,0:T(8,128)(2,1)S(1)}) custom-call(s32[3]{0:T(128)} %get-tuple-element.40.match_hbm, bf16[3,1280,256]{2,1,0:T(8,128)(2,1)} %get-tuple-element.41.inter_hbm, bf16[1280,128]{1,0:T(8,128)(2,1)} %get-tuple-element.42.user_hbm, bf16[256,128]{1,0:T(8,128)(2,1)} %get-tuple-element.43.item_hbm), custom_call_target="tpu_custom_call" | custom-call | flops 754974720 | bytes 3145728 | tf_op jit(solution)/shard_map/cond/branch_2_fun/pallas_call | solution.py:347
  179.1 0.7 copy.24
  179.8 0.6 copy.25

commit v3 on v2

--- a/solution.py
+++ b/solution.py
@@ -20,14 +20,16 @@
 FACTOR = 64.0
 CORE, Z0, Z1, Z2, Y0, Y1 = 1, 2, 4, 8, 16, 32
 HOME = 63
-MASKS = (CORE, Z0, Z1, Y0, Y1)
-STAGES = len(MASKS) + 1
+Y = Y0 | Y1
+MASKS = (CORE, Z0, Z1, Y0, Y1, Y)
+STAGES = 5
+SLOTS = STAGES + 2
 FAR = Z2
 PARTS = (
-    (0, 128, (FAR, Z1, Z0, Y1, Y0, CORE)),
-    (128, 136, (Y1, Y0, CORE, FAR, Z1, Z0)),
+    (0, 128, (FAR, Z1, Z0, Y, CORE)),
+    (128, 136, (Y, CORE, FAR, Z1, Z0)),
 )
-STAGE_TIME = {CORE: 1.0, Z0: 2.9, Z1: 3.5, FAR: 7.0, Y0: 2.9, Y1: 3.5}
+STAGE_TIME = {CORE: 1.5, Z0: 4.4, Z1: 5.2, FAR: 10.5, Y: 7.5}
 SCATTERED, SCATTER_STEP, EXCHANGED, EXCHANGE_STEP = 3.0, 1.7, 11.0, 3.5
 
 
@@ -110,7 +112,7 @@
     at_zh = (u, i ^ 1)
 
     barrier = pltpu.get_barrier_semaphore()
-    moves = MASKS + (HOME,) + tuple(sorted(set(far) - {0}))
+    moves = MASKS + (HOME,) + tuple(sorted(set(far) - {0, Z1}))
     partners = [at_user(mask) for mask in moves] + [at_x(1), at_x(2), at_x(3), at_zh]
     for partner in partners:
         pl.semaphore_signal(barrier, inc=1, device_id=partner, device_id_type=MESH)
@@ -131,16 +133,28 @@
 
     def route_part(s, part):
         first, rows, order = PARTS[part]
-        masks = tuple(far[s] if mask == FAR else mask for mask in order)
+        masks = tuple(far[s] if mask == FAR else mask for mask in order if s or mask != Z1)
         return first, rows, tuple(mask for mask in masks if mask)
 
-    def route_copy(s, part, stage):
+    def known(s, mask):
+        return mask & (FAR if s else FAR | Z1)
+
+    def route_copies(s, part, stage):
         first, rows, order = route_part(s, part)
         rows = pl.ds(first, rows)
-        return remote(
-            route_src.at[s, stage, rows], route_dst.at[s, stage, rows], route_ss.at[s],
-            route_rs.at[s, part, stage], at_user(order[stage]),
-        )
+        masks = (Y0, Y1, Y) if order[stage] == Y else (order[stage],)
+        slots = (stage, STAGES, STAGES + 1)
+        return [
+            remote(
+                route_src.at[s, stage, rows], route_dst.at[s, slot, rows], route_ss.at[s],
+                route_rs.at[s, part, slot], at_user(mask),
+            )
+            for mask, slot in zip(masks, slots)
+        ]
+
+    def route_start(s, part, stage):
+        for copy in route_copies(s, part, stage):
+            copy.start()
 
     def rs_rows(piece):
         return pl.ds(8 + piece * PIECE, PIECE) if piece else pl.ds(0, 8 + PIECE)
@@ -173,7 +187,7 @@
         for part in range(len(PARTS)):
             at = 0.0
             for stage, mask in enumerate(route_part(s, part)[2]):
-                at += STAGE_TIME[mask]
+                at += STAGE_TIME.get(mask, STAGE_TIME[FAR])
                 events.append((at, functools.partial(route_next, s, part, stage)))
         return events
 
@@ -184,17 +198,21 @@
     def route_next(s, part, stage):
         first, rows, order = route_part(s, part)
         rows = pl.ds(first, rows)
-        route_copy(s, part, stage).wait_recv()
-        if order[stage] & FAR:
+        for copy in route_copies(s, part, stage):
+            copy.wait_recv()
+        if known(s, order[stage]):
             value = route_dst[s, stage, rows]
         else:
             m0, m1 = match_ref[0], match_ref[1]
             mask = (m0, m0 ^ m1, m1 ^ HOME)[s]
-            picked = (mask & order[stage]) != 0
-            value = jnp.where(picked, route_dst[s, stage, rows], route_src[s, stage, rows])
+            picked = mask & order[stage]
+            value = jnp.where(picked != 0, route_dst[s, stage, rows], route_src[s, stage, rows])
+            if order[stage] == Y:
+                value = jnp.where(picked == Y1, route_dst[s, STAGES, rows], value)
+                value = jnp.where(picked == Y, route_dst[s, STAGES + 1, rows], value)
         if stage + 1 < len(order):
             route_src[s, stage + 1, rows] = value
-            route_copy(s, part, stage + 1).start()
+            route_start(s, part, stage + 1)
         else:
             visit[rows] = value
 
@@ -206,15 +224,17 @@
 
     pl.semaphore_wait(barrier, len(partners))
     for part in range(len(PARTS)):
-        route_copy(0, part, 0).start()
-
-    def first_users(d, total):
-        rows = pl.ds(((x + d) % 4) * QUARTER, QUARTER)
-        shp = user_ref[rows, :].astype(jnp.float32)
-        uexp[d] = exp_log(shp, jnp.ones((1, UNITS), jnp.float32), True).astype(jnp.bfloat16)
+        route_start(0, part, 0)
+
+    def first_users(n, total):
+        d, first = n // 5, pl.multiple_of((n % 5) * 64, 64)
+        shp = user_ref[pl.ds(((x + d) % 4) * QUARTER + first, 64), :].astype(jnp.float32)
+        uexp[d, pl.ds(first, 64)] = exp_log(
+            shp, jnp.ones((1, UNITS), jnp.float32), True
+        ).astype(jnp.bfloat16)
         return total + column_sum(shp)
 
-    theta = lax.fori_loop(0, 4, first_users, jnp.zeros((1, UNITS), jnp.float32))
+    theta = lax.fori_loop(0, 20, first_users, jnp.zeros((1, UNITS), jnp.float32))
     ushp[...] = user_ref[pl.ds(x * QUARTER, QUARTER), :].astype(jnp.float32)
     urte = jnp.ones((1, UNITS), jnp.float32)
 
@@ -234,32 +254,31 @@
 
         def users_of(d, first, rows):
             weights = inter[s, pl.ds(((x + d) % 4) * QUARTER + first, rows), :]
-            ue = uexp[d, first : first + rows]
+            ue = uexp[d, pl.ds(first, rows)]
             ie = iexp[...]
             denominator = lax.dot_general(
                 ue, ie, (((1,), (1,)), ((), ())), preferred_element_type=jnp.float32
             )
             ratios = (weights.astype(jnp.float32) / denominator).astype(jnp.bfloat16)
-            rs_src[s, d, 8 + first : 8 + first + rows] = ue.astype(jnp.float32) * jnp.dot(
+            rs_src[s, d, pl.ds(8 + first, rows)] = ue.astype(jnp.float32) * jnp.dot(
                 ratios, ie, preferred_element_type=jnp.float32
             )
             istat[...] += lax.dot_general(
                 ratios, ue, (((0,), (0,)), ((), ())), preferred_element_type=jnp.float32
             )
 
-        for half in range(2):
-            def users_sent(n, carry, half=half):
-                d = (n + 1) % 4
-                users_of(d, half * (QUARTER // 2), QUARTER // 2)
-
-                @pl.when(n < 3)
-                def _():
-                    for piece in range(half * PIECES // 2, (half + 1) * PIECES // 2):
-                        rs_copy(s, n + 1, piece).start()
-
-                return carry
-
-            lax.fori_loop(0, 4, users_sent, 0)
+        def users_sent(n, carry):
+            d, half = (n + 1) % 4, n // 4
+            users_of(d, pl.multiple_of(half * (QUARTER // 2), 32), QUARTER // 2)
+            for step in range(2):
+                @pl.when((d > 0) & (half == step))
+                def _(step=step):
+                    for piece in range(step * PIECES // 2, (step + 1) * PIECES // 2):
+                        rs_copy(s, d, piece).start()
+
+            return carry
+
+        lax.fori_loop(0, 8, users_sent, 0)
 
         new_rte = 0.5 * rte + 0.5 * (0.3 + FACTOR * theta)
 
@@ -278,7 +297,7 @@
         else:
             route_src[s + 1, 0, ITEMS:] = rows8(new_rte)
             for part in range(len(PARTS)):
-                route_copy(s + 1, part, 0).start()
+                route_start(s + 1, part, 0)
 
         state = {"urte": urte, "columns": jnp.zeros((1, UNITS), jnp.float32)}
 
@@ -295,15 +314,18 @@
             if piece == 0:
                 beta = zh_src[s, 0:1] + zh_dst[s, 0:1]
                 state["urte"] = 0.5 * state["urte"] + 0.5 * (0.3 + FACTOR * beta)
-            mine = pl.ds(piece * PIECE, PIECE)
-            stat = pl.ds(8 + piece * PIECE, PIECE)
-            own = 0.5 * ushp[mine] + 0.5 * (0.3 + FACTOR * (zh_src[s, stat] + zh_dst[s, stat]))
-            ushp[mine] = own
-            if last:
-                ag_src[s, mine] = log_mean(own, state["urte"])
-            else:
-                ag_src[s, mine] = exp_log(own, state["urte"])
-                state["columns"] += column_sum(own)
+            step = PIECE // 2
+
+            def own_rows(n, columns):
+                at = pl.multiple_of(piece * PIECE + n * step, 8)
+                mine, stat = pl.ds(at, step), pl.ds(at + 8, step)
+                total = zh_src[s, stat] + zh_dst[s, stat]
+                own = 0.5 * ushp[mine] + 0.5 * (0.3 + FACTOR * total)
+                ushp[mine] = own
+                ag_src[s, mine] = (log_mean if last else exp_log)(own, state["urte"])
+                return columns + column_sum(own)
+
+            state["columns"] = lax.fori_loop(0, 2, own_rows, state["columns"])
             if piece == PIECES - 1:
                 ag_src[s, QUARTER:] = rows8(state["columns"] / state["urte"])
             for step in range(1, 4):
@@ -333,7 +355,7 @@
                 theta = theta + ag_dst[s, step - 1, QUARTER : QUARTER + 1]
 
     for s in range(STRATA):
-        wait_bytes(route_src.at[s, 0 : len(route_part(s, 0)[2])], route_ss.at[s])
+        wait_bytes(route_dst.at[s, 0 : len(route_part(s, 0)[2]) + 2], route_ss.at[s])
         wait_bytes(rs_src.at[s, 1:4], rs_ss.at[s])
         wait_bytes(zh_src.at[s], zh_ss.at[s])
         wait_bytes(ag_dst.at[s], ag_ss.at[s])
@@ -358,7 +380,7 @@
             pltpu.VMEM((USERS, UNITS), jnp.bfloat16),
             pltpu.VMEM((ITEMS, UNITS), jnp.bfloat16),
             pltpu.VMEM((STRATA, STAGES, ROUTED, UNITS), f32),
-            pltpu.VMEM((STRATA, STAGES, ROUTED, UNITS), f32),
+            pltpu.VMEM((STRATA, SLOTS, ROUTED, UNITS), f32),
             pltpu.VMEM((STRATA, 4, SENT, UNITS), f32),
             pltpu.VMEM((STRATA, 3, SENT, UNITS), f32),
             pltpu.VMEM((STRATA, SENT, UNITS), f32),
@@ -374,7 +396,7 @@
             pltpu.VMEM((QUARTER, UNITS), f32),
             dma((STRATA + 3,)),
             dma((STRATA,)),
-            dma((STRATA, len(PARTS), STAGES)),
+            dma((STRATA, len(PARTS), SLOTS)),
             dma((STRATA,)),
             dma((STRATA, PIECES)),
             dma((STRATA,)),
@@ -395,13 +417,13 @@
 
 def per_device(interactions, matchings, user_shape, item_shape):
     calls = []
-    for first in range(2):
-        for second in range(2):
-            far = (first * FAR, (first ^ second) * FAR, (second ^ 1) * FAR)
+    for first in (0, Z1, Z2, Z2 | Z1):
+        for second in (0, FAR):
+            far = (first, first & FAR ^ second, second ^ FAR)
             calls.append(functools.partial(call, far, len(calls)))
-    bits = (matchings // FAR) & 1
+    first, second = matchings[0] // Z1 & 3, matchings[1] // FAR & 1
     return lax.switch(
-        bits[0] * 2 + bits[1], calls, interactions, matchings, user_shape, item_shape
+        first * 2 + second, calls, interactions, matchings, user_shape, item_shape
     )
 
 

time: 181 us -> 153 us (0.85)
  the two profiles are of different devices: /device:TPU:104 before, /device:TPU:96 now
where the time goes in v3:
time: 153 us
  Pallas kernels  144 us (94%)
  between operations  5.85 us (4%)
  local copies, waits for them, and re-layouts  2.67 us (2%)
    pallas_call x1, Pallas kernels, call(): pl.pallas_call(functools.partial(kernel, far), out_shape=(jax.ShapeDtypeS...  144 us

profile of v3, /device:TPU:96, one launch (start us, length us, event | category | flops | bytes accessed | tf_op | source)
XLA Modules:
  0.0 153.1 jit_solution(8860689165274104989)
XLA Ops:
  0.6 1.3 fusion
  7.2 144.6 %conditional.1 = ((bf16[1280,128]{1,0:T(8,128)(2,1)S(1)}, bf16[256,128]{1,0:T(8,128)(2,1)S(1)})) conditional(s32[]{:T(128)} %clamp.3, (s32[3]{0:T(128)}, bf16[3,1280,256]{2,1,0:T(8,128)(2,1)}, bf16[1280,128]{1,0:T(8,128)(2,1)}, bf16[256,128]{1,0:T(8,128)(2,1)}) %tuple.31, (s32[3]{0:T(128)}, ...), branch_computations={%region_0.1_spmd, %region_1.2_spmd, %region_2.3_spmd, %region_3.4_... | conditional | flops 754974720 | bytes 3145736 | solution.py:425
  7.4 144.4 %branch_5_fun.1 = (bf16[1280,128]{1,0:T(8,128)(2,1)S(1)}, bf16[256,128]{1,0:T(8,128)(2,1)S(1)}) custom-call(s32[3]{0:T(128)} %get-tuple-element.84.match_hbm, bf16[3,1280,256]{2,1,0:T(8,128)(2,1)} %get-tuple-element.85.inter_hbm, bf16[1280,128]{1,0:T(8,128)(2,1)} %get-tuple-element.86.user_hbm, bf16[256,128]{1,0:T(8,128)(2,1)} %get-tuple-element.87.item_hbm), custom_call_target="tpu_custom_call" | custom-call | flops 754974720 | bytes 3145728 | tf_op jit(solution)/shard_map/cond/branch_5_fun/pallas_call | solution.py:369
  151.8 0.7 copy.40
  152.5 0.6 copy.41

commit v4 on v3

--- a/solution.py
+++ b/solution.py
@@ -26,8 +26,8 @@
 SLOTS = STAGES + 2
 FAR = Z2
 PARTS = (
-    (0, 128, (FAR, Z1, Z0, Y, CORE)),
-    (128, 136, (Y, CORE, FAR, Z1, Z0)),
+    (0, 128, (FAR, Y, Z1, Z0, CORE)),
+    (128, 136, (Y, Z0, Z1, FAR, CORE)),
 )
 STAGE_TIME = {CORE: 1.5, Z0: 4.4, Z1: 5.2, FAR: 10.5, Y: 7.5}
 SCATTERED, SCATTER_STEP, EXCHANGED, EXCHANGE_STEP = 3.0, 1.7, 11.0, 3.5
@@ -421,10 +421,9 @@
         for second in (0, FAR):
             far = (first, first & FAR ^ second, second ^ FAR)
             calls.append(functools.partial(call, far, len(calls)))
-    first, second = matchings[0] // Z1 & 3, matchings[1] // FAR & 1
-    return lax.switch(
-        first * 2 + second, calls, interactions, matchings, user_shape, item_shape
-    )
+    bits = (matchings // jnp.array((Z1, Z2, 1))) & jnp.array((3, 1, 0))
+    chosen = jnp.sum(bits * jnp.array((2, 1, 0)))
+    return lax.switch(chosen, calls, interactions, matchings, user_shape, item_shape)
 
 
 def solution(mesh):

time: 153 us -> 150 us (0.980); the launches traced: 153 us -> 148 us
  between operations: 5.85 us -> 1.29 us
where the time goes in v4:
time: 150 us; the launch traced here: 148 us
  Pallas kernels  144 us (96%)
    pallas_call x1, Pallas kernels, call(): pl.pallas_call(functools.partial(kernel, far), out_shape=(jax.ShapeDtypeS...  144 us

profile of v4, /device:TPU:96, one launch (start us, length us, event | category | flops | bytes accessed | tf_op | source)
XLA Modules:
  0.0 148.5 jit_solution(2579109632759134101)
XLA Ops:
  0.6 1.5 multiply_reduce_fusion
  2.8 144.3 %conditional.1 = ((bf16[1280,128]{1,0:T(8,128)(2,1)S(1)}, bf16[256,128]{1,0:T(8,128)(2,1)S(1)})) conditional(s32[]{:T(128)} %clamp.3, (s32[3]{0:T(128)}, bf16[3,1280,256]{2,1,0:T(8,128)(2,1)}, bf16[1280,128]{1,0:T(8,128)(2,1)}, bf16[256,128]{1,0:T(8,128)(2,1)}) %tuple.31, (s32[3]{0:T(128)}, ...), branch_computations={%region_1.2_spmd, %region_2.3_spmd, %region_3.4_spmd, %region_4.5_... | conditional | flops 754974720 | bytes 3145736 | solution.py:426
  2.8 144.1 %branch_0_fun.1 = (bf16[1280,128]{1,0:T(8,128)(2,1)S(1)}, bf16[256,128]{1,0:T(8,128)(2,1)S(1)}) custom-call(s32[3]{0:T(128)} %get-tuple-element.64.match_hbm, bf16[3,1280,256]{2,1,0:T(8,128)(2,1)} %get-tuple-element.65.inter_hbm, bf16[1280,128]{1,0:T(8,128)(2,1)} %get-tuple-element.66.user_hbm, bf16[256,128]{1,0:T(8,128)(2,1)} %get-tuple-element.67.item_hbm), custom_call_target="tpu_custom_call" | custom-call | flops 754974720 | bytes 3145728 | tf_op jit(solution)/shard_map/cond/branch_0_fun/pallas_call | solution.py:369
  147.1 0.7 copy.43
  147.8 0.6 copy.44
